TPU v7x, 32 devices: a whole 2x2x4 slice. The times are simulated.
32 devices in a mesh: grp: 2 (over y), gy: 4 (over z), gz: 4 (over x, core).
Axes of the slice: x: 2, y: 2, z: 4, core: 2. Of those that a mesh axis runs over, the one named last changes fastest.
Arguments:
- snapshots: bfloat16 [512, 8, 16, 128], P('grp', 'gy', 'gz'), parts along dimension 0, may hold values from -12.5 to 12.5
- fluid_mask: int32 [16, 16, 128], P(('grp', 'gy'), 'gz'), parts along dimension 0, may hold values 0 or 1
Outputs:
- modes: float32 [512, 8, 16, 128], P('grp', 'gy', 'gz'), parts along dimension 0
- factor: float32 [512, 256], P('grp'), parts along dimension 0
There are 2 independent parts, one for each index of `grp`. A program takes and returns all parts, laid end to end along the dimension named above; each array names one. Nothing has to cross between parts.
All inputs are finite; a program needn't handle non-finite values. No bound on the sum of `fluid_mask` on one device may be relied on, other than what follows from the above.
Results may differ from a plain program's by a relative error of at most 0.0003.
Values may be sent and summed in bfloat16 or wider, within the bound.
A program may use at most 64 MiB of HBM per device.

v0:
```python
import math
import jax
import jax.numpy as jnp
from jax import lax
from jax.sharding import PartitionSpec as P

gauss_taps = (0.05448868, 0.24420134, 0.40261995, 0.24420134, 0.05448868)


def with_halo(cells, sides, width):
    for axis, dim in sides:
        count = lax.axis_size(axis)
        ends = count - 1
        head = lax.slice_in_dim(cells, 0, width, axis=dim)
        tail = lax.slice_in_dim(cells, cells.shape[dim] - width, cells.shape[dim], axis=dim)
        cells = jnp.concatenate(
            [
                lax.ppermute(tail, axis, [(i, (i + 1) % count) for i in range(ends)]),
                cells,
                lax.ppermute(head, axis, [((i + 1) % count, i) for i in range(ends)]),
            ],
            axis=dim,
        )
    return cells


def filter_inner(field, axis, length):
    total = gauss_taps[0] * lax.slice_in_dim(field, 0, length, axis=axis)
    for offset in range(1, 5):
        total = total + gauss_taps[offset] * lax.slice_in_dim(
            field, offset, offset + length, axis=axis
        )
    return total


def filter_edge(field, axis):
    widths = [(0, 0)] * field.ndim
    widths[axis] = (2, 2)
    return filter_inner(jnp.pad(field, widths), axis, field.shape[axis])


def cholesky_pair(gram):
    count = gram.shape[0]
    places = jnp.arange(count, dtype=jnp.int32)

    def column_step(index, carry):
        upper, inverse = carry
        index = jnp.asarray(index).astype(jnp.int32)
        column = lax.dynamic_slice_in_dim(upper, index, 1, 1)[:, 0]
        grow = lax.dynamic_slice_in_dim(gram, index, 1, 0)[0]
        rest = grow - jnp.dot(column, upper, precision=lax.Precision.HIGHEST)
        pick = (places == index).astype(jnp.float32)
        pivot = jnp.sqrt(jnp.sum(rest * pick))
        row_new = jnp.where(places >= index, rest, jnp.float32(0.0)) / pivot
        upper = upper + pick[:, None] * row_new[None, :]
        inv_col = (pick - jnp.dot(inverse, column, precision=lax.Precision.HIGHEST)) / pivot
        inverse = inverse + inv_col[:, None] * pick[None, :]
        return (upper, inverse)

    start = jnp.zeros((count, count), jnp.float32)
    return lax.fori_loop(0, count, column_step, (start, start))


def total_factor(matrix):
    gram = jnp.dot(matrix, matrix.T, precision=lax.Precision.HIGHEST)
    summed = lax.psum(gram, ("gy", "gz"))
    return cholesky_pair(summed)


def body(snapshots, fluid_mask):
    cells_y = snapshots.shape[1]
    cells_z = snapshots.shape[2]
    extended = with_halo(snapshots, (("gy", 1),), 2)
    field = filter_inner(filter_edge(extended.astype(jnp.float32), 3), 1, cells_y)
    widened = with_halo(field, (("gz", 2),), 2)
    field = filter_inner(widened, 2, cells_z)
    field = field * fluid_mask.astype(jnp.float32)[None]
    matrix = field.reshape(field.shape[0], -1)
    scale = math.sqrt(matrix.shape[1] * lax.axis_size("gy") * lax.axis_size("gz"))
    first, first_inv = total_factor(matrix)
    basis = jnp.dot(first_inv.T, matrix, precision=lax.Precision.HIGHEST)
    second, second_inv = total_factor(basis)
    ortho = jnp.dot(second_inv.T, basis, precision=lax.Precision.HIGHEST)
    modes = (ortho * scale).reshape(snapshots.shape)
    factor = jnp.dot(second, first, precision=lax.Precision.HIGHEST) / scale
    return (modes, factor)


def solution(mesh):
    placed = (P("grp", "gy", "gz", None), P(("grp", "gy"), "gz", None))
    return jax.shard_map(
        body,
        mesh=mesh,
        in_specs=placed,
        out_specs=(P("grp", "gy", "gz", None), P("grp", None)),
        check_vma=False,
    )
```

profile of v0, /device:TPU:1, one launch (start us, length us, event | category | flops | bytes accessed | tf_op | source)
XLA Modules:
  0.0 1758.6 jit_solution(4903046267069832524)
XLA Ops:
  7.2 1.3 copy.11
  8.5 4.1 collective-permute-start
  12.6 1.3 collective-permute-start.1
  13.9 9.2 collective-permute-done
  23.1 3.8 collective-permute-done.1
  27.2 1.8 multiply_add_fusion.4
  29.6 4.9 collective-permute-start.2
  34.7 1.9 collective-permute-start.3
  36.7 4.0 collective-permute-done.2
  40.8 4.5 collective-permute-done.3
  45.3 1.2 copy.17
  46.9 2.5 convolution_bitcast_fusion
  49.6 88.4 %all-reduce.4.cloned.1.call-done = f32[256,256]{1,0:T(8,128)} async-done(((f32[256,256]{1,0:T(8,128)}), f32[256,256]{1,0:T(8,128)}) %all-reduce.4.cloned.1.call-update) | async-done | bytes 262160 | tf_op jit(solution)/shard_map/psum | solution.py:66
  137.9 758.4 %while.34 = (s32[]{:T(128)}, f32[256,256]{0,1:T(8,128)S(1)}, f32[256,256]{1,0:T(8,128)S(1)}, f32[256,256]{1,0:T(8,128)}, s32[]{:T(128)}, /*index=5*/s32[]{:T(128)}) while((s32[]{:T(128)}, f32[256,256]{0,1:T(8,128)S(1)}, f32[256,256]{1,0:T(8,128)S(1)}, f32[256,256]{1,0:T(8,128)}, s32[]{:T(128)}, ...), condition=%wide.region_3.4_spmd.clone.clone, body=%wide.region_1.3_spmd.clone.clone.sunk | while | flops 2100738 | bytes 2115706 | solution.py:61
  141.2 0.8 constant_dynamic-slice_fusion.16
  156.0 0.8 constant_dynamic-slice_fusion.16
  176.7 0.8 constant_dynamic-slice_fusion.16
  896.3 1.9 fusion.41
  898.2 1.7 fusion.42
  900.0 89.5 %all-reduce.6.cloned.1.call-done = f32[256,256]{1,0:T(8,128)} async-done(((f32[256,256]{1,0:T(8,128)}), f32[256,256]{1,0:T(8,128)}) %all-reduce.6.cloned.1.call-update) | async-done | bytes 262160 | tf_op jit(solution)/shard_map/psum | solution.py:66
  989.4 758.5 %while.35 = (s32[]{:T(128)}, f32[256,256]{0,1:T(8,128)S(1)}, f32[256,256]{1,0:T(8,128)S(1)}, f32[256,256]{1,0:T(8,128)}, s32[]{:T(128)}, /*index=5*/s32[]{:T(128)}) while((s32[]{:T(128)}, f32[256,256]{0,1:T(8,128)S(1)}, f32[256,256]{1,0:T(8,128)S(1)}, f32[256,256]{1,0:T(8,128)}, s32[]{:T(128)}, ...), condition=%wide.region_7.8_spmd.clone.clone, body=%wide.region_5.7_spmd.clone.clone.sunk | while | flops 2100738 | bytes 2115706 | solution.py:61
  1748.0 1.0 convolution_multiply_fusion
  1749.0 1.4 reshape.40
  1750.5 1.3 convolution_multiply_fusion.1
  (4623 shorter events, 1131.6 us)
Async XLA Ops:
  7.2 130.8 %all-reduce.4.cloned.1.call-start = ((), (), s32[]{:S(2)}) async-start(), calls=%async_computation | async-start | bytes 524288 | tf_op jit(solution)/shard_map/psum | solution.py:66
  8.5 14.6 collective-permute-start
  12.6 14.4 collective-permute-start.1
  29.3 7.3 copy-start
  29.6 11.0 collective-permute-start.2
  34.7 10.6 collective-permute-start.3
  49.5 940.0 %all-reduce.6.cloned.1.call-start = ((), (), s32[]{:S(2)}) async-start(), calls=%async_computation.1 | async-start | bytes 524288 | tf_op jit(solution)/shard_map/psum | solution.py:66
Sparse Core Ops, SparseCore 0:
  49.6 88.2 all-reduce.3
  900.1 89.3 all-reduce.5
where the time goes:
time: 1790 us; the launch traced here: 1760 us
  other arithmetic  470 us (26%)
  local copies, waits for them, and re-layouts  396 us (22%)
  loops' own time  385 us (22%)
  matrix products  282 us (16%)
  waiting for transfers between devices  199 us (11%)
    dynamic_slice x512, local copies, waits for them, and re-layouts, column_step(): grow = lax.dynamic_slice_in_dim(gram, index, 1, 0)[0]  391 us
    another operation x2, loops' own time, cholesky_pair(): return lax.fori_loop(0, count, column_step, (start, start))  385 us
    reduce_sum x512, other arithmetic, column_step(): pivot = jnp.sqrt(jnp.sum(rest * pick))  309 us
    psum x2, waiting for transfers between devices, total_factor(): summed = lax.psum(gram, ('gy', 'gz'))  178 us
    dot_general x512, matrix products, column_step(): jnp.dot(inverse, column, precision=lax.Precision.HIGHEST)  138 us
    dot_general x512, matrix products, column_step(): rest = grow - jnp.dot(column, upper, precision=lax.Precision.HIGHEST)  136 us
    add x512, other arithmetic, column_step(): upper = upper + pick[:, None] * row_new[None, :]  57.4 us
    add x512, other arithmetic, column_step(): inverse = inverse + inv_col[:, None] * pick[None, :]  57.3 us

commit v1 on v0

--- a/solution.py
+++ b/solution.py
@@ -63,7 +63,7 @@
 
 def total_factor(matrix):
     gram = jnp.dot(matrix, matrix.T, precision=lax.Precision.HIGHEST)
-    summed = lax.psum(gram, ("gy", "gz"))
+    summed = jnp.sum(lax.all_gather(gram, ("gy", "gz")), axis=0)
     return cholesky_pair(summed)
 
 

time: 1790 us -> 1330 us (0.74); the launches traced: 1760 us -> 1330 us
  local copies, waits for them, and re-layouts: 396 us -> 35.4 us
  waiting for transfers between devices: 199 us -> 120 us
    dynamic_slice x512, local copies, waits for them, and re-layouts: 391 us -> 31.8 us  [column_step(): grow = lax.dynamic_slice_in_dim(gram, index, 1, 0)[0]]
    psum x2 -> x0, waiting for transfers between devices: 178 us -> none  [total_factor(): summed = lax.psum(gram, ('gy', 'gz'))]
    all_gather x0 -> x2, waiting for transfers between devices: none -> 98.8 us  [total_factor(): summed = jnp.sum(lax.all_gather(gram, ('gy', 'gz')), axis=0)]
where the time goes in v1:
time: 1330 us
  other arithmetic  475 us (36%)
  loops' own time  389 us (29%)
  matrix products  282 us (21%)
  waiting for transfers between devices  120 us (9%)
  local copies, waits for them, and re-layouts  35.4 us (3%)
  between operations  14.2 us (1%)
    another operation x2, loops' own time, cholesky_pair(): return lax.fori_loop(0, count, column_step, (start, start))  389 us
    reduce_sum x512, other arithmetic, column_step(): pivot = jnp.sqrt(jnp.sum(rest * pick))  308 us
    dot_general x512, matrix products, column_step(): jnp.dot(inverse, column, precision=lax.Precision.HIGHEST)  138 us
    dot_general x512, matrix products, column_step(): rest = grow - jnp.dot(column, upper, precision=lax.Precision.HIGHEST)  136 us
    all_gather x2, waiting for transfers between devices, total_factor(): summed = jnp.sum(lax.all_gather(gram, ('gy', 'gz')), axis=0)  98.8 us
    add x512, other arithmetic, column_step(): upper = upper + pick[:, None] * row_new[None, :]  57.4 us
    add x512, other arithmetic, column_step(): inverse = inverse + inv_col[:, None] * pick[None, :]  57.1 us
    dynamic_slice x512, local copies, waits for them, and re-layouts, column_step(): grow = lax.dynamic_slice_in_dim(gram, index, 1, 0)[0]  31.8 us

profile of v1, /device:TPU:1, one launch (start us, length us, event | category | flops | bytes accessed | tf_op | source)
XLA Modules:
  0.0 1327.8 jit_solution(4880376849529426003)
XLA Ops:
  7.2 1.3 copy.11
  8.5 4.1 collective-permute-start
  12.6 1.3 collective-permute-start.1
  13.9 9.2 collective-permute-done
  23.1 3.8 collective-permute-done.1
  27.2 1.8 multiply_add_fusion.4
  29.6 4.9 collective-permute-start.2
  34.7 1.9 collective-permute-start.3
  36.7 4.0 collective-permute-done.2
  40.8 4.4 collective-permute-done.3
  45.8 2.5 convolution_bitcast_fusion
  48.6 49.6 %all-gather.5.cloned.1.call-done = f32[4096,256]{1,0:T(8,128)} async-done(((f32[256,256]{1,0:T(8,128)}), f32[4096,256]{1,0:T(8,128)}) %all-gather.5.cloned.1.call-update) | async-done | bytes 4194320 | tf_op jit(solution)/shard_map/all_gather | solution.py:66
  98.2 2.5 reduce_sum.44
  100.7 580.6 %while.34 = (s32[]{:T(128)}, f32[256,256]{0,1:T(8,128)S(1)}, f32[256,256]{1,0:T(8,128)S(1)}, f32[256,256]{1,0:T(8,128)S(1)}, s32[]{:T(128)}, /*index=5*/s32[]{:T(128)}) while((s32[]{:T(128)}, f32[256,256]{0,1:T(8,128)S(1)}, f32[256,256]{1,0:T(8,128)S(1)}, f32[256,256]{1,0:T(8,128)S(1)}, s32[]{:T(128)}, ...), condition=%wide.region_3.4_spmd.clone.clone, body=%wide.region_1.3_spmd.clone.clone.sunk | while | flops 2100738 | bytes 2115706 | solution.py:61
  105.6 0.6 fusion.72
  114.7 0.6 fusion.72
  681.3 1.9 fusion.41
  683.2 1.7 fusion.42
  684.9 49.2 %all-gather.7.cloned.1.call-done = f32[4096,256]{1,0:T(8,128)} async-done(((f32[256,256]{1,0:T(8,128)}), f32[4096,256]{1,0:T(8,128)}) %all-gather.7.cloned.1.call-update) | async-done | bytes 4194320 | tf_op jit(solution)/shard_map/all_gather | solution.py:66
  734.1 2.5 reduce_sum.45
  736.6 580.6 %while.35 = (s32[]{:T(128)}, f32[256,256]{0,1:T(8,128)S(1)}, f32[256,256]{1,0:T(8,128)S(1)}, f32[256,256]{1,0:T(8,128)S(1)}, s32[]{:T(128)}, /*index=5*/s32[]{:T(128)}) while((s32[]{:T(128)}, f32[256,256]{0,1:T(8,128)S(1)}, f32[256,256]{1,0:T(8,128)S(1)}, f32[256,256]{1,0:T(8,128)S(1)}, s32[]{:T(128)}, ...), condition=%wide.region_7.8_spmd.clone.clone, body=%wide.region_5.7_spmd.clone.clone.sunk | while | flops 2100738 | bytes 2115706 | solution.py:61
  1317.2 1.0 convolution_multiply_fusion
  1318.2 1.4 reshape.40
  1319.7 1.3 convolution_multiply_fusion.1
  (4625 shorter events, 773.5 us)
Async XLA Ops:
  7.2 91.1 %all-gather.5.cloned.1.call-start = ((), (), s32[]{:S(2)}) async-start(), calls=%async_computation | async-start | bytes 4456448 | tf_op jit(solution)/shard_map/all_gather | solution.py:66
  8.5 14.6 %collective-permute-start = (bf16[256,2,4,128]{0,3,2,1:T(8,128)(2,1)S(1)}, bf16[256,2,4,128]{0,3,2,1:T(8,128)(2,1)S(1)}, u32[]{:S(2)}, u32[]{:S(2)}) collective-permute-start(bf16[256,2,4,128]{0,3,2,1:T(8,128)(2,1)S(1)} %copy.11), channel_id=1, source_target_pairs={{0,4},{4,8},{8,12},{1,5},{5,9},{9,13},{2,6},{6,10},{10,14},{3,7},{... | collective-permute-start | bytes 1572872 | tf_op jit(solution)/shard_map/ppermute | solution.py:18
  12.6 14.4 %collective-permute-start.1 = (bf16[256,2,4,128]{0,3,2,1:T(8,128)(2,1)S(1)}, bf16[256,2,4,128]{0,3,2,1:T(8,128)(2,1)S(1)}, u32[]{:S(2)}, u32[]{:S(2)}) collective-permute-start(bf16[256,2,4,128]{0,3,2,1:T(8,128)(2,1)S(1)} %copy.11), channel_id=1, source_target_pairs={{4,0},{8,4},{12,8},{5,1},{9,5},{13,9},{6,2},{10,6},{14,10},{7,3},{... | collective-permute-start | bytes 1572872 | tf_op jit(solution)/shard_map/ppermute | solution.py:20
  29.3 7.3 copy-start
  29.6 11.0 collective-permute-start.2
  34.7 10.5 collective-permute-start.3
  48.3 685.8 %all-gather.7.cloned.1.call-start = ((), (), s32[]{:S(2)}) async-start(), calls=%async_computation.1 | async-start | bytes 4456448 | tf_op jit(solution)/shard_map/all_gather | solution.py:66
Sparse Core Ops, SparseCore 0:
  48.5 49.7 all-gather.4
  685.0 49.0 all-gather.6
